TPU v7x, 32 devices: a whole 2x2x4 slice. The times are simulated.
32 devices in a mesh: tp: 8 (over y, x, core), sp: 4 (over z).
Axes of the slice: x: 2, y: 2, z: 4, core: 2. Of those that a mesh axis runs over, the one named last changes fastest.
Arguments:
- inputs: bfloat16 [256, 8192], P('tp', 'sp'), may hold values from -6 to 6
- out_grad: bfloat16 [256, 8192], P('sp', 'tp'), may hold values from -6 to 6
- gate_pre: bfloat16 [256, 28672], P(None, 'tp'), may hold values from -6 to 6
- up_pre: bfloat16 [256, 28672], P(None, 'tp'), may hold values from -6 to 6
- w_gate: bfloat16 [8192, 28672], P('sp', 'tp'), may hold values from -0.0625 to 0.0625
- w_up: bfloat16 [8192, 28672], P('sp', 'tp'), may hold values from -0.0625 to 0.0625
- w_down: bfloat16 [28672, 8192], P('tp', 'sp'), may hold values from -0.03125 to 0.03125
Outputs:
- grad_input: bfloat16 [256, 8192], P('tp', 'sp')
- grad_gate: bfloat16 [8192, 28672], P('sp', 'tp')
- grad_up: bfloat16 [8192, 28672], P('sp', 'tp')
- grad_down: bfloat16 [28672, 8192], P('tp', 'sp')
All inputs are finite; a program needn't handle non-finite values.
Results may differ from a plain program's by a relative error of at most 0.0049.
Values may be sent and summed in bfloat16 or wider, within the bound.
A program may use at most 192 MiB of HBM per device.

v0:
```python
import jax
import jax.numpy as jnp
from jax import lax
from jax.sharding import PartitionSpec as P


def swiglu_back(hidden_grad, gate_pre, up_pre):
    gate = gate_pre.astype(jnp.float32)
    upward = up_pre.astype(jnp.float32)
    sigmoid = jax.nn.sigmoid(gate)
    up_grad = (hidden_grad * gate * sigmoid).astype(jnp.bfloat16)
    gate_grad = (hidden_grad * upward * sigmoid * (1.0 + gate * (1.0 - sigmoid))).astype(
        jnp.bfloat16
    )
    return (gate_grad, up_grad)


def rows_times(grads, weight):
    return lax.dot_general(
        grads, weight, (((1,), (1,)), ((), ())), preferred_element_type=jnp.float32
    )


def per_device(inputs, out_grad, gate_pre, up_pre, w_gate, w_up, w_down):
    wide_rows = lax.all_gather(out_grad, "tp", axis=1, tiled=True)
    regrouped = lax.all_to_all(wide_rows, "sp", split_axis=1, concat_axis=0, tiled=True)
    gate = gate_pre.astype(jnp.float32)
    hidden = (gate * jax.nn.sigmoid(gate) * up_pre.astype(jnp.float32)).astype(jnp.bfloat16)
    grad_down = lax.dot_general(
        hidden, regrouped, (((0,), (0,)), ((), ())), preferred_element_type=jnp.float32
    ).astype(jnp.bfloat16)
    partial_grad = lax.dot_general(
        regrouped, w_down, (((1,), (1,)), ((), ())), preferred_element_type=jnp.float32
    )
    hidden_grad = lax.psum(partial_grad, "sp")
    gate_grad, up_grad = swiglu_back(hidden_grad, gate_pre, up_pre)
    dims = (((0,), (0,)), ((), ()))
    piece = lax.all_gather(inputs, "tp", axis=0, tiled=True)
    new_gate = lax.dot_general(piece, gate_grad, dims, preferred_element_type=jnp.float32)
    new_up = lax.dot_general(piece, up_grad, dims, preferred_element_type=jnp.float32)
    via_gate = lax.psum_scatter(
        rows_times(gate_grad, w_gate), "tp", scatter_dimension=0, tiled=True
    )
    via_up = lax.psum_scatter(rows_times(up_grad, w_up), "tp", scatter_dimension=0, tiled=True)
    total = via_gate + via_up
    return (
        total.astype(jnp.bfloat16),
        new_gate.astype(jnp.bfloat16),
        new_up.astype(jnp.bfloat16),
        grad_down,
    )


def solution(mesh):
    in_specs = (
        P("tp", "sp"),
        P("sp", "tp"),
        P(None, "tp"),
        P(None, "tp"),
        P("sp", "tp"),
        P("sp", "tp"),
        P("tp", "sp"),
    )
    out_specs = (P("tp", "sp"), P("sp", "tp"), P("sp", "tp"), P("tp", "sp"))
    return jax.shard_map(
        per_device, mesh=mesh, in_specs=in_specs, out_specs=out_specs, check_vma=False
    )
```

profile of v0, /device:TPU:0, one launch (start us, length us, event | category | flops | bytes accessed | tf_op | source)
XLA Modules:
  0.0 316.0 jit_solution(610266666883076665)
XLA Ops:
  7.2 0.0 all-gather.3.cloned.1.call-start
  7.2 0.7 all-gather.3.cloned.1.call-update
  7.9 0.0 all-reduce.2.cloned.1.call-start
  7.9 28.2 %all-gather.3.cloned.1.call-done = bf16[64,8192]{1,0:T(8,128)(2,1)} async-done(((bf16[64,1024]{1,0:T(8,128)(2,1)}), bf16[64,8192]{1,0:T(8,128)(2,1)}) %all-gather.3.cloned.1.call-update) | async-done | bytes 1048592 | tf_op jit(solution)/shard_map/all_gather | solution.py:25
  36.1 1.3 copy.23
  37.4 30.6 %all_to_all.19 = bf16[64,4,2048]{2,0,1:T(8,128)(2,1)S(1)} all-to-all(bf16[64,4,2048]{2,0,1:T(8,128)(2,1)S(1)} %bitcast.20), channel_id=1, replica_groups=mesh['tp'=8,'sp'=4] {'sp'}, dimensions={1} | all-to-all | bytes 2097152 | tf_op jit(solution)/shard_map/all_to_all | solution.py:26
  68.0 9.1 %fusion.17 = f32[256,3584]{1,0:T(8,128)} fusion(bf16[256,2048]{1,0:T(8,128)(2,1)S(1)} %bitcast.21, bf16[3584,2048]{1,0:T(8,128)(2,1)} %param.13), kind=kOutput, calls=%fused_computation.25 | convolution fusion | flops 3758096384 | bytes 19398656 | tf_op jit(solution)/shard_map/dot_general | solution.py:32
  77.1 0.0 all-reduce.2.cloned.1.call-update
  77.1 0.0 all-gather.5.cloned.1.call-start
  77.2 0.7 all-gather.5.cloned.1.call-update
  77.9 0.0 reduce-scatter.2.cloned.1.call-start
  77.9 135.5 %all-reduce.2.cloned.1.call-done = f32[256,3584]{1,0:T(8,128)} async-done(((f32[256,3584]{1,0:T(8,128)}), f32[256,3584]{1,0:T(8,128)}) %all-reduce.2.cloned.1.call-update) | async-done | bytes 3670032 | tf_op jit(solution)/shard_map/psum | solution.py:35
  213.5 4.6 %fusion.4 = bf16[256,3584]{1,0:T(8,128)(2,1)S(1)} fusion(f32[256,3584]{1,0:T(8,128)} %all-reduce.2.cloned.1.call-done, bf16[256,3584]{1,0:T(8,128)(2,1)} %param.10, bf16[256,3584]{1,0:T(8,128)(2,1)} %param.9), kind=kLoop, calls=%fused_computation.13 | loop fusion | flops 11010048 | bytes 9175040 | tf_op jit(solution)/shard_map/convert_element_type | solution.py:12
  218.1 8.9 %fusion.18 = f32[256,2048]{1,0:T(8,128)} fusion(bf16[256,3584]{1,0:T(8,128)(2,1)S(1)} %fusion.4, bf16[2048,3584]{1,0:T(8,128)(2,1)} %param.11), kind=kOutput, calls=%fused_computation.26 | convolution fusion | flops 3758096384 | bytes 18612224 | tf_op jit(solution)/shard_map/dot_general | solution.py:19
  227.1 12.9 %convolution_add_fusion = f32[256,2048]{1,0:T(8,128)} fusion(f32[256,2048]{1,0:T(8,128)} %fusion.18, bf16[2048,3584]{1,0:T(8,128)(2,1)} %param.12, f32[256,3584]{1,0:T(8,128)} %all-reduce.2.cloned.1.call-done, bf16[256,3584]{1,0:T(8,128)(2,1)} %param.9), kind=kOutput, calls=%fused_computation.21 | convolution fusion | flops 3765043200 | bytes 24379392 | tf_op jit(solution)/shard_map/dot_general | solution.py:19
  240.0 0.0 reduce-scatter.2.cloned.1.call-update
  240.0 10.3 %convolution_convert_fusion = bf16[3584,2048]{1,0:T(8,128)(2,1)} fusion(bf16[256,2048]{1,0:T(8,128)(2,1)S(1)} %bitcast.22, bf16[256,3584]{1,0:T(8,128)(2,1)} %param.10, bf16[256,3584]{1,0:T(8,128)(2,1)} %param.9), kind=kOutput, calls=%fused_computation | convolution fusion | flops 3772776448 | bytes 19398656 | tf_op jit(solution)/shard_map/dot_general | solution.py:29
  250.3 0.0 all-gather.5.cloned.1.call-done
  250.3 12.9 %fusion.1 = bf16[2048,3584]{0,1:T(8,128)(2,1)} fusion(bf16[256,2048]{1,0:T(8,128)(2,1)} %all-gather.5.cloned.1.call-done, f32[256,3584]{1,0:T(8,128)} %all-reduce.2.cloned.1.call-done, bf16[256,3584]{1,0:T(8,128)(2,1)} %param.9), kind=kOutput, calls=%fused_computation.4 | convolution fusion | flops 3771858944 | bytes 21233664 | tf_op jit(solution)/shard_map/dot_general | solution.py:40
  263.2 0.0 copy-start
  263.2 18.8 %copy.20 = bf16[2048,3584]{1,0:T(8,128)(2,1)} copy(bf16[2048,3584]{0,1:T(8,128)(2,1)} %fusion.1) | data formatting | bytes 29360128
  281.9 0.0 copy-done
  281.9 7.3 %fusion = bf16[2048,3584]{0,1:T(8,128)(2,1)} fusion(bf16[256,3584]{1,0:T(8,128)(2,1)S(1)} %fusion.4, bf16[256,2048]{1,0:T(8,128)(2,1)S(1)} %copy-done), kind=kOutput, calls=%fused_computation.3 | convolution fusion | flops 3765436416 | bytes 17563648 | tf_op jit(solution)/shard_map/dot_general | solution.py:39
  289.2 18.6 %copy.19 = bf16[2048,3584]{1,0:T(8,128)(2,1)} copy(bf16[2048,3584]{0,1:T(8,128)(2,1)} %fusion) | data formatting | bytes 29360128
  307.9 0.0 reduce-scatter.2.cloned.1.call-done
  307.9 1.6 convert_element_type.39
Async XLA Ops:
  7.2 29.0 %all-gather.3.cloned.1.call-start = ((), (), s32[]{:S(2)}) async-start(), calls=%async_computation.2 | async-start | bytes 1179648 | tf_op jit(solution)/shard_map/all_gather | solution.py:25
  7.9 205.6 %all-reduce.2.cloned.1.call-start = ((), (), s32[]{:S(2)}) async-start(), calls=%async_computation.3 | async-start | bytes 7340032 | tf_op jit(solution)/shard_map/psum | solution.py:35
  77.1 173.1 %all-gather.5.cloned.1.call-start = ((), (), s32[]{:S(2)}) async-start(), calls=%async_computation.4 | async-start | bytes 1179648 | tf_op jit(solution)/shard_map/all_gather | solution.py:38
  77.9 230.0 %reduce-scatter.2.cloned.1.call-start = ((), (), s32[]{:S(2)}) async-start(), calls=%async_computation.5 | async-start | bytes 2359296 | tf_op jit(solution)/shard_map/reduce_scatter | solution.py:41
  263.2 18.8 %copy-start = (bf16[256,2048]{1,0:T(8,128)(2,1)S(1)}, bf16[256,2048]{1,0:T(8,128)(2,1)}, u32[]{:S(2)}) copy-start(bf16[256,2048]{1,0:T(8,128)(2,1)} %all-gather.5.cloned.1.call-done) | copy-start | bytes 3145732
Sparse Core Ops, SparseCore 0:
  9.9 26.1 all-gather.2
  77.3 136.1 all-reduce.1
  215.4 22.4 all-gather.4
  241.0 41.1 reduce-scatter.1
where the time goes:
time: 317 us; the launch traced here: 316 us
  waiting for transfers between devices  165 us (52%)
  matrix products  61.5 us (19%)
  local copies, waits for them, and re-layouts  38.7 us (12%)
  blocking collectives  30.6 us (10%)
  between operations  13.8 us (4%)
  other arithmetic  6.26 us (2%)
    psum x1, waiting for transfers between devices, per_device(): hidden_grad = lax.psum(partial_grad, 'sp')  136 us
    unnamed x4, local copies, waits for them, and re-layouts  37.4 us
    all_to_all x1, blocking collectives, per_device(): lax.all_to_all(wide_rows, 'sp', split_axis=1, concat_axis=0, tiled=True)  30.6 us
    all_gather x1, waiting for transfers between devices, per_device(): wide_rows = lax.all_gather(out_grad, 'tp', axis=1, tiled=True)  28.2 us
    dot_general x2, matrix products, rows_times(): lax.dot_general(grads, weight, (((1,), (1,)), ((), ())), preferred_elemen...  21.9 us
    dot_general x1, matrix products, per_device(): lax.dot_general(piece, up_grad, dims, preferred_element_type=jnp.float32)  12.9 us
    dot_general x1, matrix products, per_device(): lax.dot_general(hidden, regrouped, (((0,), (0,)), ((), ())), preferred_el...  10.3 us
    dot_general x1, matrix products, per_device(): lax.dot_general(regrouped, w_down, (((1,), (1,)), ((), ())), preferred_el...  9.13 us
  transfers between devices with their start and end apart: 4, of which 2 were waited for; matrix products, arithmetic and copies ran while one was open for 30% of the time, Pallas kernels for 0%

commit v1 on v0

--- a/solution.py
+++ b/solution.py
@@ -32,7 +32,11 @@
     partial_grad = lax.dot_general(
         regrouped, w_down, (((1,), (1,)), ((), ())), preferred_element_type=jnp.float32
     )
-    hidden_grad = lax.psum(partial_grad, "sp")
+    hidden_grad = partial_grad
+    for hop in (1, 2):
+        hidden_grad = hidden_grad + lax.ppermute(
+            hidden_grad, "sp", [(dev, dev ^ hop) for dev in range(4)]
+        )
     gate_grad, up_grad = swiglu_back(hidden_grad, gate_pre, up_pre)
     dims = (((0,), (0,)), ((), ()))
     piece = lax.all_gather(inputs, "tp", axis=0, tiled=True)

time: 317 us -> 417 us (1.32)
  waiting for transfers between devices: 165 us -> 267 us
  matrix products: 61.5 us -> 55 us
    ppermute x0 -> x2, waiting for transfers between devices: none -> 238 us  [per_device(): lax.ppermute(hidden_grad, 'sp', [(dev, dev ^ hop) for dev in range(4)])]
    psum x1 -> x0, waiting for transfers between devices: 136 us -> none  [per_device(): hidden_grad = lax.psum(partial_grad, 'sp')]
    dot_general x1, matrix products: 12.9 us -> 7.3 us  [per_device(): lax.dot_general(piece, up_grad, dims, preferred_element_type=jnp.float32)]
    unnamed x4 -> x6, local copies, waits for them, and re-layouts: 37.4 us -> 37.4 us
  transfers between devices with their start and end apart: 4 -> 5, of which waited for: 2 -> 3; matrix products, arithmetic and copies ran while one was open for 30% -> 22% of each run, Pallas kernels for 0% -> 0%
where the time goes in v1:
time: 417 us; the launch traced here: 416 us
  waiting for transfers between devices  267 us (64%)
  matrix products  55 us (13%)
  local copies, waits for them, and re-layouts  38.7 us (9%)
  blocking collectives  30.6 us (7%)
  between operations  13.8 us (3%)
  other arithmetic  9.24 us (2%)
    ppermute x2, waiting for transfers between devices, per_device(): lax.ppermute(hidden_grad, 'sp', [(dev, dev ^ hop) for dev in range(4)])  238 us
    unnamed x6, local copies, waits for them, and re-layouts  37.4 us
    all_to_all x1, blocking collectives, per_device(): lax.all_to_all(wide_rows, 'sp', split_axis=1, concat_axis=0, tiled=True)  30.6 us
    all_gather x1, waiting for transfers between devices, per_device(): wide_rows = lax.all_gather(out_grad, 'tp', axis=1, tiled=True)  28.2 us
    dot_general x2, matrix products, rows_times(): lax.dot_general(grads, weight, (((1,), (1,)), ((), ())), preferred_elemen...  18.8 us
    dot_general x1, matrix products, per_device(): lax.dot_general(piece, gate_grad, dims, preferred_element_type=jnp.float32)  11.4 us
    dot_general x1, matrix products, per_device(): lax.dot_general(hidden, regrouped, (((0,), (0,)), ((), ())), preferred_el...  10.2 us
  transfers between devices with their start and end apart: 5, of which 3 were waited for; matrix products, arithmetic and copies ran while one was open for 22% of the time, Pallas kernels for 0%

profile of v1, /device:TPU:0, one launch (start us, length us, event | category | flops | bytes accessed | tf_op | source)
XLA Modules:
  0.0 415.8 jit_solution(1893886229625268471)
XLA Ops:
  7.2 0.0 all-gather.3.cloned.1.call-start
  7.2 0.7 all-gather.3.cloned.1.call-update
  7.9 0.0 all-gather.5.cloned.1.call-start
  7.9 28.2 %all-gather.3.cloned.1.call-done = bf16[64,8192]{1,0:T(8,128)(2,1)} async-done(((bf16[64,1024]{1,0:T(8,128)(2,1)}), bf16[64,8192]{1,0:T(8,128)(2,1)}) %all-gather.3.cloned.1.call-update) | async-done | bytes 1048592 | tf_op jit(solution)/shard_map/all_gather | solution.py:25
  36.1 1.3 copy.23
  37.4 30.6 %all_to_all.19 = bf16[64,4,2048]{2,0,1:T(8,128)(2,1)S(1)} all-to-all(bf16[64,4,2048]{2,0,1:T(8,128)(2,1)S(1)} %bitcast.22), channel_id=1, replica_groups=mesh['tp'=8,'sp'=4] {'sp'}, dimensions={1} | all-to-all | bytes 2097152 | tf_op jit(solution)/shard_map/all_to_all | solution.py:26
  68.0 7.3 %fusion.16 = f32[256,3584]{1,0:T(8,128)S(1)} fusion(bf16[256,2048]{1,0:T(8,128)(2,1)S(1)} %bitcast.23, bf16[3584,2048]{1,0:T(8,128)(2,1)} %param.13), kind=kOutput, calls=%fused_computation.25 | convolution fusion | flops 3758096384 | bytes 19398656 | tf_op jit(solution)/shard_map/dot_general | solution.py:32
  75.3 0.3 collective-permute-start
  75.6 80.2 %collective-permute-done = f32[256,3584]{1,0:T(8,128)S(1)} collective-permute-done((f32[256,3584]{1,0:T(8,128)S(1)}, f32[256,3584]{1,0:T(8,128)S(1)}, u32[]{:S(2)}, u32[]{:S(2)}) %collective-permute-start) | collective-permute-done | bytes 3670048 | tf_op jit(solution)/shard_map/ppermute | solution.py:37
  155.8 2.4 add.20
  158.2 0.6 collective-permute-start.1
  158.8 0.0 all-gather.5.cloned.1.call-update
  158.8 0.2 reduce-scatter.2.cloned.1.call-start
  159.0 158.3 %collective-permute-done.1 = f32[256,3584]{1,0:T(8,128)} collective-permute-done((f32[256,3584]{1,0:T(8,128)}, f32[256,3584]{1,0:T(8,128)}, u32[]{:S(2)}, u32[]{:S(2)}) %collective-permute-start.1) | collective-permute-done | bytes 3670048 | tf_op jit(solution)/shard_map/ppermute | solution.py:37
  317.3 5.2 %fusion.11 = (bf16[256,3584]{1,0:T(8,128)(2,1)S(1)}, bf16[256,3584]{1,0:T(8,128)(2,1)S(1)}) fusion(bf16[256,3584]{1,0:T(8,128)(2,1)} %param.9, f32[256,3584]{1,0:T(8,128)} %add.20, f32[256,3584]{1,0:T(8,128)} %collective-permute-done.1, bf16[256,3584]{1,0:T(8,128)(2,1)} %param.10), kind=kLoop, calls=%fused_computation.20 | loop fusion | flops 14680064 | bytes 14680064 | tf_op jit(solution)/shard_map/convert_element_type | solution.py:11
  322.5 0.0 copy-start
  322.5 9.3 %fusion.17 = f32[256,2048]{1,0:T(8,128)} fusion(bf16[256,3584]{1,0:T(8,128)(2,1)S(1)} %get-tuple-element.20, bf16[2048,3584]{1,0:T(8,128)(2,1)} %param.12), kind=kOutput, calls=%fused_computation.26 | convolution fusion | flops 3758096384 | bytes 18612224 | tf_op jit(solution)/shard_map/dot_general | solution.py:19
  331.8 0.0 copy-done
  331.8 9.5 %fusion.15 = f32[256,2048]{1,0:T(8,128)} fusion(f32[256,2048]{1,0:T(8,128)} %fusion.17, bf16[256,3584]{1,0:T(8,128)(2,1)S(1)} %get-tuple-element.21, bf16[2048,3584]{1,0:T(8,128)(2,1)} %param.11), kind=kOutput, calls=%fused_computation.24 | convolution fusion | flops 3758620672 | bytes 20709376 | tf_op jit(solution)/shard_map/dot_general | solution.py:19
  341.3 0.0 reduce-scatter.2.cloned.1.call-update
  341.4 10.2 %convolution_convert_fusion = bf16[3584,2048]{1,0:T(8,128)(2,1)} fusion(bf16[256,2048]{1,0:T(8,128)(2,1)S(1)} %bitcast.24, bf16[256,3584]{1,0:T(8,128)(2,1)} %param.10, bf16[256,3584]{1,0:T(8,128)(2,1)} %param.9), kind=kOutput, calls=%fused_computation | convolution fusion | flops 3772776448 | bytes 19398656 | tf_op jit(solution)/shard_map/dot_general | solution.py:29
  351.6 0.0 all-gather.5.cloned.1.call-done
  351.6 11.4 %fusion = bf16[2048,3584]{0,1:T(8,128)(2,1)} fusion(bf16[256,3584]{1,0:T(8,128)(2,1)} %copy-done, bf16[256,2048]{1,0:T(8,128)(2,1)} %all-gather.5.cloned.1.call-done), kind=kOutput, calls=%fused_computation.3 | convolution fusion | flops 3765436416 | bytes 17563648 | tf_op jit(solution)/shard_map/dot_general | solution.py:43
  362.9 0.0 copy-start.1
  362.9 18.8 %copy.19 = bf16[2048,3584]{1,0:T(8,128)(2,1)} copy(bf16[2048,3584]{0,1:T(8,128)(2,1)} %fusion) | data formatting | bytes 29360128
  381.7 0.0 copy-done.1
  381.7 7.3 %fusion.1 = bf16[2048,3584]{0,1:T(8,128)(2,1)} fusion(bf16[256,3584]{1,0:T(8,128)(2,1)S(1)} %get-tuple-element.20, bf16[256,2048]{1,0:T(8,128)(2,1)S(1)} %copy-done.1), kind=kOutput, calls=%fused_computation.4 | convolution fusion | flops 3765436416 | bytes 17563648 | tf_op jit(solution)/shard_map/dot_general | solution.py:44
  389.0 18.6 %copy.20 = bf16[2048,3584]{1,0:T(8,128)(2,1)} copy(bf16[2048,3584]{0,1:T(8,128)(2,1)} %fusion.1) | data formatting | bytes 29360128
  407.6 0.0 reduce-scatter.2.cloned.1.call-done
  407.6 1.6 convert_element_type.39
Async XLA Ops:
  7.2 29.0 %all-gather.3.cloned.1.call-start = ((), (), s32[]{:S(2)}) async-start(), calls=%async_computation.2 | async-start | bytes 1179648 | tf_op jit(solution)/shard_map/all_gather | solution.py:25
  7.9 343.7 %all-gather.5.cloned.1.call-start = ((), (), s32[]{:S(2)}) async-start(), calls=%async_computation.3 | async-start | bytes 1179648 | tf_op jit(solution)/shard_map/all_gather | solution.py:42
  75.3 80.4 %collective-permute-start = (f32[256,3584]{1,0:T(8,128)S(1)}, f32[256,3584]{1,0:T(8,128)S(1)}, u32[]{:S(2)}, u32[]{:S(2)}) collective-permute-start(f32[256,3584]{1,0:T(8,128)S(1)} %fusion.16), channel_id=1, source_target_pairs={{0,1},{1,0},{2,3},{3,2},{4,5},{5,4},{6,7},{7,6},{8,9},{9,8},{10,11... | collective-permute-start | bytes 11010056 | tf_op jit(solution)/shard_map/ppermute | solution.py:37
  158.2 159.1 %collective-permute-start.1 = (f32[256,3584]{1,0:T(8,128)}, f32[256,3584]{1,0:T(8,128)}, u32[]{:S(2)}, u32[]{:S(2)}) collective-permute-start(f32[256,3584]{1,0:T(8,128)} %add.20), channel_id=1, source_target_pairs={{0,2},{1,3},{2,0},{3,1},{4,6},{5,7},{6,4},{7,5},{8,10},{9,11},{10,... | collective-permute-start | bytes 11010056 | tf_op jit(solution)/shard_map/ppermute | solution.py:37
  158.8 248.8 %reduce-scatter.2.cloned.1.call-start = ((), (), s32[]{:S(2)}) async-start(), calls=%async_computation.4 | async-start | bytes 2359296 | tf_op jit(solution)/shard_map/reduce_scatter | solution.py:45
  322.5 9.3 %copy-start = (bf16[256,3584]{1,0:T(8,128)(2,1)}, bf16[256,3584]{1,0:T(8,128)(2,1)S(1)}, u32[]{:S(2)}) copy-start(bf16[256,3584]{1,0:T(8,128)(2,1)S(1)} %get-tuple-element.21) | copy-start | bytes 5505028
  362.9 18.8 %copy-start.1 = (bf16[256,2048]{1,0:T(8,128)(2,1)S(1)}, bf16[256,2048]{1,0:T(8,128)(2,1)}, u32[]{:S(2)}) copy-start(bf16[256,2048]{1,0:T(8,128)(2,1)} %all-gather.5.cloned.1.call-done) | copy-start | bytes 3145732
Sparse Core Ops, SparseCore 0:
  9.9 26.1 all-gather.2
  158.9 22.4 all-gather.4
  341.5 39.9 reduce-scatter.1
